TPU v7x, 1024 devices: a whole 8x8x8 slice. The times are simulated.
1024 devices in a mesh: outer: 64 (over z_lo, y, core), inner: 16 (over x, z_hi).
Axes of the slice: x: 8, y: 8, z: 8 (z_hi: 2, z_lo: 4; z = z_hi * 4 + z_lo), core: 2. Of those that a mesh axis runs over, the one named last changes fastest.
Arguments:
- hidden: bfloat16 [4096, 14336], P('inner', 'outer'), may hold values from -6 to 6
- grad_out: bfloat16 [4096, 6144], P('inner', 'outer'), may hold values from -0.29882812 to 0.29882812
- codes: bfloat16 [14336, 6144], P('outer', 'inner'), may hold values from -4 to 4
- scales: float32 [14336, 48], P('outer', 'inner'), may hold values from 0.1 to 0.6
Outputs:
- grad_hidden: bfloat16 [4096, 14336], P('inner', 'outer')
- grad_weight: float32 [14336, 6144], P('outer', 'inner')
All inputs are finite; a program needn't handle non-finite values.
Results may differ from a plain program's by a relative error of at most 0.017.
Values may be sent and summed in bfloat16 or wider, within the bound.
A program may use at most 32 MiB of HBM per device.

v0:
```python
import jax
import jax.numpy as jnp
from jax import lax
from jax.sharding import PartitionSpec as P

BLK = 128


def shards(hidden, grad_out, codes, scales):
    full_grad = lax.all_gather(grad_out, "outer", axis=1, tiled=True)
    local_weight = (codes.astype(jnp.float32) * jnp.repeat(scales, BLK, axis=1)).astype(
        jnp.bfloat16
    )
    weight = lax.all_gather(local_weight, "inner", axis=1, tiled=True)
    grad_hidden = lax.dot_general(
        full_grad, weight, (((1,), (1,)), ((), ())), preferred_element_type=jnp.float32
    )
    term = lax.dot_general(
        hidden, full_grad, (((0,), (0,)), ((), ())), preferred_element_type=jnp.float32
    )
    grad_weight = lax.psum_scatter(
        term.astype(jnp.bfloat16), "inner", scatter_dimension=1, tiled=True
    ).astype(jnp.float32)
    return (grad_hidden.astype(jnp.bfloat16), grad_weight)


def solution(mesh):
    return jax.shard_map(
        shards,
        mesh=mesh,
        in_specs=(
            P("inner", "outer"),
            P("inner", "outer"),
            P("outer", "inner"),
            P("outer", "inner"),
        ),
        out_specs=(P("inner", "outer"), P("outer", "inner")),
        check_vma=False,
    )
```

profile of v0, /device:TPU:20, one launch (start us, length us, event | category | flops | bytes accessed | tf_op | source)
XLA Modules:
  0.0 524.0 jit_solution(3178335971223217598)
XLA Ops:
  7.2 0.0 copy-start
  7.2 0.0 all-gather.5.cloned.1.call-start
  7.2 0.7 all-gather.5.cloned.1.call-update
  7.9 0.0 all-gather.3.cloned.1.call-start
  8.0 1.1 copy.8
  9.0 1.4 fusion.1
  10.4 0.0 all-gather.3.cloned.1.call-update
  10.4 0.0 reduce-scatter.4.cloned.1.call-start
  10.5 133.2 %all-gather.5.cloned.1.call-done = bf16[256,6144]{0,1:T(8,128)(2,1)} async-done(((bf16[256,96]{0,1:T(8,128)(2,1)}), bf16[256,6144]{0,1:T(8,128)(2,1)}) %all-gather.5.cloned.1.call-update) | async-done | bytes 3145744 | tf_op jit(solution)/shard_map/all_gather | solution.py:10
  143.7 0.0 copy-done
  143.7 3.0 convolution_convert_fusion
  146.7 2.9 copy.9
  149.6 0.0 copy-start.1
  149.6 0.0 reduce-scatter.4.cloned.1.call-update
  149.6 123.1 %all-gather.3.cloned.1.call-done = bf16[224,6144]{0,1:T(8,128)(2,1)} async-done(((bf16[224,384]{0,1:T(8,128)(2,1)}), bf16[224,6144]{0,1:T(8,128)(2,1)}) %all-gather.3.cloned.1.call-update) | async-done | bytes 2752528 | tf_op jit(solution)/shard_map/all_gather | solution.py:14
  272.7 0.0 copy-done.1
  272.7 3.6 fusion
  276.3 239.2 %reduce-scatter.4.cloned.1.call-done = bf16[384,224]{1,0:T(8,128)(2,1)} async-done(((bf16[6144,224]{1,0:T(8,128)(2,1)}), bf16[384,224]{1,0:T(8,128)(2,1)}) %reduce-scatter.4.cloned.1.call-update) | async-done | bytes 172048
  515.6 1.1 copy.10
  516.7 0.8 convert_element_type.23
Async XLA Ops:
  7.2 136.5 %copy-start = (bf16[256,224]{0,1:T(8,128)(2,1)S(1)}, bf16[256,224]{0,1:T(8,128)(2,1)}, u32[]{:S(2)}) copy-start(bf16[256,224]{0,1:T(8,128)(2,1)} %param.4) | copy-start | bytes 344068
  7.2 136.5 %all-gather.5.cloned.1.call-start = ((), (), s32[]{:S(2)}) async-start(), calls=%async_computation.2 | async-start | bytes 3194880 | tf_op jit(solution)/shard_map/all_gather | solution.py:10
  7.9 264.8 %all-gather.3.cloned.1.call-start = ((), (), s32[]{:S(2)}) async-start(), calls=%async_computation.1 | async-start | bytes 3342336 | tf_op jit(solution)/shard_map/all_gather | solution.py:14
  10.4 505.1 %reduce-scatter.4.cloned.1.call-start = ((), (), s32[]{:S(2)}) async-start(), calls=%async_computation.3 | async-start | bytes 3342336
  149.6 123.1 %copy-start.1 = (bf16[256,6144]{0,1:T(8,128)(2,1)S(1)}, bf16[256,6144]{0,1:T(8,128)(2,1)}, u32[]{:S(2)}) copy-start(bf16[256,6144]{0,1:T(8,128)(2,1)} %all-gather.5.cloned.1.call-done) | copy-start | bytes 9437188
Sparse Core Ops, SparseCore 0:
  10.7 132.9 all-gather.4
  148.6 124.0 all-gather.2
  278.5 237.0 reduce-scatter.3
where the time goes:
time: 524 us
  waiting for transfers between devices  496 us (95%)
  between operations  13.8 us (3%)
  matrix products  6.68 us (1%)
    unnamed x4, waiting for transfers between devices  240 us
    all_gather x1, waiting for transfers between devices, shards(): full_grad = lax.all_gather(grad_out, 'outer', axis=1, tiled=True)  133 us
    all_gather x1, waiting for transfers between devices, shards(): weight = lax.all_gather(local_weight, 'inner', axis=1, tiled=True)  123 us
  transfers between devices with their start and end apart: 3, of which 3 were waited for; matrix products, arithmetic and copies ran while one was open for 2% of the time, Pallas kernels for 0%

commit v1 on v0

v1 whole, which is shorter than its diff:
```python
import jax
import jax.numpy as jnp
from jax import lax
from jax.experimental import pallas as pl
from jax.experimental.pallas import tpu as pltpu
from jax.sharding import PartitionSpec as P

BLK = 128
X, HZ, ZL, Y = 8, 2, 4, 8
TOK, FFD, GCOL, WCOL = 256, 224, 96, 384
MESH = pl.DeviceIdType.MESH
F32, BF16 = jnp.float32, jnp.bfloat16


def kernel(
    ht, gt, codes, scales, ght, gw,
    g, hb, w, acc, p, rs_out, rs_in, gw_out, gw_in,
    perm_s, perm_r, z_s, z_r, y_s, y_r, sib_s, sib_r, h_s, h_r, w_s, w_r, rs_s, rs_r, gw_s, gw_r,
):
    o = lax.axis_index("outer")
    i = lax.axis_index("inner")
    c = lax.rem(o, 2)
    y = lax.rem(o // 2, Y)
    zl = o // (2 * Y)
    x = i // HZ
    h = lax.rem(i, HZ)
    sgn = 1 - 2 * c

    def dev(x_, h_, zl_, y_, c_):
        return {"outer": zl_ * (2 * Y) + y_ * 2 + c_, "inner": x_ * HZ + h_}

    def mod(a, n):
        return lax.rem(a + n, n)

    perm_to = dev(2 * zl + y // 4, h, mod(lax.rem(y, 4) + 2, 4), x, c)
    perm_from = dev(y, h, x // 2, lax.rem(x, 2) * 4 + mod(zl + 2, 4), c)
    z_peer = [dev(x, h, mod(zl + r, ZL), y, c) for r in range(1, ZL)]
    sibling = dev(x, h, zl, y, 1 - c)
    y_long, y_short = dev(x, h, zl, mod(y + sgn, Y), c), dev(x, h, zl, mod(y - sgn, Y), c)
    x_long, x_short = dev(mod(x + sgn, X), h, zl, y, c), dev(mod(x - sgn, X), h, zl, y, c)
    h_peer = dev(x, 1 - h, zl, y, c)
    peers = [perm_to, perm_from, *z_peer, sibling, y_long, y_short, x_long, x_short, h_peer]

    barrier = pltpu.get_barrier_semaphore()
    for peer in peers:
        pl.semaphore_signal(barrier, inc=1, device_id=peer, device_id_type=MESH)

    for b in range(WCOL // BLK):
        cols = slice(b * BLK, (b + 1) * BLK)
        scale = jnp.broadcast_to(scales[b : b + 1, :], (BLK, FFD)).T
        w[h, :, cols] = (codes[:, cols].astype(F32) * scale).astype(BF16)
    hb[x] = ht[...]

    pl.semaphore_wait(barrier, len(peers))

    sends = []

    def copy(src, dst, s, r, to):
        return pltpu.make_async_remote_copy(
            src_ref=src, dst_ref=dst, send_sem=s, recv_sem=r, device_id=to, device_id_type=MESH
        )

    def start(cp):
        cp.start()
        sends.append(cp)

    def chunk(t, k):
        return g.at[t, mod(zl + 2 - k, 4), c]

    def y_block(d, s):
        return mod(y - sgn * s, Y) if d == 0 else mod(y + sgn * s, Y)

    def x_block(d, s):
        return mod(x - sgn * s, X) if d == 0 else mod(x + sgn * s, X)

    def ring(d, s, k):
        ref = chunk(y_block(d, s), k)
        return copy(ref, ref, y_s.at[d, s, k], y_r.at[d, s, k], y_long if d == 0 else y_short)

    def sib(t, k):
        ref = chunk(t, k)
        return copy(ref, ref, sib_s.at[t, k], sib_r.at[t, k], sibling)

    def hcopy(d, s):
        ref = hb.at[x_block(d, s)]
        return copy(ref, ref, h_s.at[d, s], h_r.at[d, s], x_long if d == 0 else x_short)

    steps = (4, 3)

    def h_step(s):
        for d in (0, 1):
            if s < steps[d]:
                hcopy(d, s).wait_recv()
                if s + 1 < steps[d]:
                    start(hcopy(d, s + 1))

    perm = copy(gt, g.at[x, lax.rem(y, 4), c], perm_s, perm_r, perm_to)
    start(perm)
    for d in (0, 1):
        start(hcopy(d, 0))

    def zcopy(k):
        ref = chunk(y, 0)
        return copy(ref, ref, z_s.at[k - 1], z_r.at[k - 1], z_peer[k - 1])

    for k in range(4):
        if k == 0:
            perm.wait_recv()
            for r in range(1, 4):
                start(zcopy(r))
        else:
            zcopy(k).wait_recv()
        start(ring(0, 0, k))
        start(ring(1, 0, k))
        start(sib(y, k))
        if k == 0:
            h_step(0)
    w_copy = copy(w.at[h], w.at[h], w_s, w_r, h_peer)
    start(w_copy)
    h_step(1)

    def grad_hidden(t):
        for k in range(4):
            sib(t, k).wait_recv()
        r = lax.dot_general(
            w[0], g[t, 0:2].reshape(WCOL, TOK), (((1,), (0,)), ((), ())), preferred_element_type=F32
        )
        p[t] = r + lax.dot_general(
            w[1], g[t, 2:4].reshape(WCOL, TOK), (((1,), (0,)), ((), ())), preferred_element_type=F32
        )

    def grad_weight(t, first=False):
        for n in range(2):
            r = lax.dot_general(
                hb[t],
                g[t, 2 * n : 2 * n + 2].reshape(WCOL, TOK),
                (((1,), (1,)), ((), ())),
                preferred_element_type=F32,
            )
            if first:
                acc[n] = r
            else:
                acc[n] += r

    def at_distance(s):
        return [y_block(0, s)] if s in (0, 4) else [y_block(0, s), y_block(1, s)]

    for s in range(4):
        for k in range(4):
            for d in (0, 1):
                if s < steps[d]:
                    ring(d, s, k).wait_recv()
                    if s + 1 < steps[d]:
                        start(ring(d, s + 1, k))
                    start(sib(y_block(d, s + 1), k))
        if s < 2:
            h_step(s + 2)
        if s == 1:
            w_copy.wait_recv()
            for t in at_distance(0) + at_distance(1):
                grad_hidden(t)
            grad_weight(y, True)
            for t in at_distance(1):
                grad_weight(t)
        if s >= 2:
            for t in at_distance(s):
                grad_hidden(t)
                grad_weight(t)
    grad_hidden(y_block(0, 4))
    grad_weight(y_block(0, 4))

    gw_out[...] = acc[1 - h].astype(BF16)
    gw_copy = copy(gw_out, gw_in, gw_s, gw_r, h_peer)
    start(gw_copy)

    half = FFD // 2

    def rs(d, e, q):
        rows = pl.ds(q * half, half)
        return copy(
            rs_out.at[d, e, rows], rs_in.at[d, e, rows], rs_s.at[d, e, q], rs_r.at[d, e, q],
            x_long if d == 0 else x_short,
        )

    for e in range(4):
        for q in range(2):
            rows = pl.ds(q * half, half)
            for d in (0, 1):
                if e < steps[d]:
                    b = mod(x + sgn * (4 - e), X) if d == 0 else mod(x - sgn * (3 - e), X)
                    v = p[b, rows]
                    if e > 0:
                        rs(d, e - 1, q).wait_recv()
                        v = v + rs_in[d, e - 1, rows].astype(F32)
                    rs_out[d, e, rows] = v.astype(BF16)
                    start(rs(d, e, q))
    for q in range(2):
        rows = pl.ds(q * half, half)
        rs(1, 2, q).wait_recv()
        v = p[x, rows] + rs_in[1, 2, rows].astype(F32)
        rs(0, 3, q).wait_recv()
        ght[rows] = (v + rs_in[0, 3, rows].astype(F32)).astype(BF16)
    gw_copy.wait_recv()
    gw[...] = acc[h] + gw_in[...].astype(F32)
    for cp in sends:
        cp.wait_send()


def shards(hidden, grad_out, codes, scales):
    vmem = pl.BlockSpec(memory_space=pltpu.VMEM)
    dma = pltpu.SemaphoreType.DMA
    ght, gw = pl.pallas_call(
        kernel,
        out_shape=(
            jax.ShapeDtypeStruct((FFD, TOK), BF16),
            jax.ShapeDtypeStruct((FFD, WCOL), F32),
        ),
        in_specs=[vmem] * 4,
        out_specs=(vmem, vmem),
        scratch_shapes=[
            pltpu.VMEM((Y, 4, 2, GCOL, TOK), BF16),
            pltpu.VMEM((X, FFD, TOK), BF16),
            pltpu.VMEM((2, FFD, WCOL), BF16),
            pltpu.VMEM((2, FFD, WCOL), F32),
            pltpu.VMEM((X, FFD, TOK), F32),
            pltpu.VMEM((2, 4, FFD, TOK), BF16),
            pltpu.VMEM((2, 4, FFD, TOK), BF16),
            pltpu.VMEM((FFD, WCOL), BF16),
            pltpu.VMEM((FFD, WCOL), BF16),
            dma, dma,
            dma((3,)), dma((3,)),
            dma((2, 4, 4)), dma((2, 4, 4)),
            dma((8, 4)), dma((8, 4)),
            dma((2, 4)), dma((2, 4)),
            dma, dma,
            dma((2, 4, 2)), dma((2, 4, 2)),
            dma, dma,
        ],
        compiler_params=pltpu.CompilerParams(
            collective_id=0, has_side_effects=True, vmem_limit_bytes=40 * 2**20
        ),
        name="fused",
    )(hidden.T, grad_out.T, codes, scales.T)
    return ght.T, gw


def solution(mesh):
    return jax.shard_map(
        shards,
        mesh=mesh,
        in_specs=(
            P("inner", "outer"),
            P("inner", "outer"),
            P("outer", "inner"),
            P("outer", "inner"),
        ),
        out_specs=(P("inner", "outer"), P("outer", "inner")),
        check_vma=False,
    )
```

time: 524 us -> 83.5 us (0.16)
  the two profiles are of different devices: /device:TPU:20 before, /device:TPU:2 now
where the time goes in v1:
time: 83.5 us; the launch traced here: 83.2 us
  Pallas kernels  77.9 us (93%)
  local copies, waits for them, and re-layouts  4.67 us (6%)
    pallas_call x1, Pallas kernels, shards(): pl.pallas_call(kernel, out_shape=(jax.ShapeDtypeStruct((FFD, TOK), BF16),...  77.9 us
    unnamed x10, local copies, waits for them, and re-layouts  4.67 us

profile of v1, /device:TPU:2, one launch (start us, length us, event | category | flops | bytes accessed | tf_op | source)
XLA Modules:
  0.0 83.2 jit_solution(9408114181746310647)
XLA Ops:
  0.6 0.0 copy-start.3
  0.6 0.7 copy-done.3
  1.3 0.0 copy-start
  1.3 0.9 %copy-done = bf16[224,384]{1,0:T(8,128)(2,1)S(1)} copy-done((bf16[224,384]{1,0:T(8,128)(2,1)S(1)}, bf16[224,384]{1,0:T(8,128)(2,1)}, u32[]{:S(2)}) %copy-start) | copy-done | bytes 172056
  2.2 0.0 copy-start.1
  2.2 0.9 %copy-done.1 = bf16[256,224]{0,1:T(8,128)(2,1)S(1)} copy-done((bf16[256,224]{0,1:T(8,128)(2,1)S(1)}, bf16[256,224]{0,1:T(8,128)(2,1)}, u32[]{:S(2)}) %copy-start.1) | copy-done | bytes 114712
  3.1 0.0 copy-start.2
  3.1 0.8 copy-done.2
  3.9 77.9 %fused.1 = (bf16[224,256]{1,0:T(8,128)(2,1)S(1)}, f32[224,384]{1,0:T(8,128)S(1)}) custom-call(bf16[224,256]{1,0:T(8,128)(2,1)S(1)} %bitcast.5, bf16[96,256]{1,0:T(8,128)(2,1)S(1)} %bitcast.6, bf16[224,384]{1,0:T(8,128)(2,1)S(1)} %copy-done, f32[3,224]{1,0:T(4,128)S(1)} %bitcast.7), custom_call_target="tpu_custom_call" | custom-call | tf_op jit(solution)/shard_map/fused/pallas_call | solution.py:212
  81.8 0.6 copy.8
  82.5 0.7 copy.9
Async XLA Ops:
  0.6 0.7 copy-start.3
  1.3 0.9 %copy-start = (bf16[224,384]{1,0:T(8,128)(2,1)S(1)}, bf16[224,384]{1,0:T(8,128)(2,1)}, u32[]{:S(2)}) copy-start(bf16[224,384]{1,0:T(8,128)(2,1)} %codes.1) | copy-start | bytes 516100
  2.2 0.9 %copy-start.1 = (bf16[256,224]{0,1:T(8,128)(2,1)S(1)}, bf16[256,224]{0,1:T(8,128)(2,1)}, u32[]{:S(2)}) copy-start(bf16[256,224]{0,1:T(8,128)(2,1)} %param.4) | copy-start | bytes 344068
  3.1 0.8 copy-start.2

commit v2 on v1

v2 whole, which is shorter than its diff:
```python
import jax
import jax.numpy as jnp
from jax import lax
from jax.experimental import pallas as pl
from jax.experimental.pallas import tpu as pltpu
from jax.sharding import PartitionSpec as P

BLK = 128
X, HZ, ZL, Y = 8, 2, 4, 8
TOK, FFD, GCOL, WCOL = 256, 224, 96, 384
MESH = pl.DeviceIdType.MESH
F32, BF16 = jnp.float32, jnp.bfloat16


def kernel(
    ht, gt, codes, scales, ght, gw,
    g, hb, cv, sv, w, acc, p, rs_out, pair_in, own_in, gw_out, gw_in,
    in_s, perm_s, perm_r, z_s, z_r, y_s, y_r, sib_s, sib_r, last_s, last_r, h_s, h_r, w_s, w_r, rs_s, pair_r, own_r, gw_s, gw_r,
):
    o = lax.axis_index("outer")
    i = lax.axis_index("inner")
    c = lax.rem(o, 2)
    y = lax.rem(o // 2, Y)
    zl = o // (2 * Y)
    x = i // HZ
    h = lax.rem(i, HZ)
    sgn = 1 - 2 * c

    def dev(x_, h_, zl_, y_, c_):
        return {"outer": zl_ * (2 * Y) + y_ * 2 + c_, "inner": x_ * HZ + h_}

    def mod(a, n):
        return lax.rem(a + n, n)

    perm_to = dev(2 * zl + y // 4, h, mod(lax.rem(y, 4) + 2, 4), x, c)
    perm_from = dev(y, h, x // 2, lax.rem(x, 2) * 4 + mod(zl + 2, 4), c)
    z_peer = [dev(x, h, mod(zl + r, ZL), y, c) for r in range(1, ZL)]
    sibling = dev(x, h, zl, y, 1 - c)
    y_long, y_short = dev(x, h, zl, mod(y + sgn, Y), c), dev(x, h, zl, mod(y - sgn, Y), c)
    x_long, x_short = dev(mod(x + sgn, X), h, zl, y, c), dev(mod(x - sgn, X), h, zl, y, c)
    h_peer = dev(x, 1 - h, zl, y, c)
    x_far = [dev(mod(x + n * sgn, X), h, zl, y, c) for n in (3, -3, 2, -2)]
    peers = [perm_to, perm_from, *z_peer, sibling, y_long, y_short, x_long, x_short, *x_far, h_peer]

    barrier = pltpu.get_barrier_semaphore()
    for peer in peers:
        pl.semaphore_signal(barrier, inc=1, device_id=peer, device_id_type=MESH)

    loads = [
        pltpu.make_async_copy(codes, cv, in_s.at[0]),
        pltpu.make_async_copy(scales, sv, in_s.at[1]),
        pltpu.make_async_copy(ht, hb.at[x], in_s.at[2]),
    ]
    for load in loads:
        load.start()

    pl.semaphore_wait(barrier, len(peers))

    sends = []

    def copy(src, dst, s, r, to):
        return pltpu.make_async_remote_copy(
            src_ref=src, dst_ref=dst, send_sem=s, recv_sem=r, device_id=to, device_id_type=MESH
        )

    def start(cp):
        cp.start()
        sends.append(cp)

    def chunk(t, k):
        return g.at[t, mod(zl + 2 - k, 4), c]

    def y_block(d, s):
        return mod(y - sgn * s, Y) if d == 0 else mod(y + sgn * s, Y)

    def x_block(d, s):
        return mod(x - sgn * s, X) if d == 0 else mod(x + sgn * s, X)

    def ring(d, s, k):
        ref = chunk(y_block(d, s), k)
        return copy(ref, ref, y_s.at[d, s, k], y_r.at[d, s, k], y_long if d == 0 else y_short)

    def sib(t):
        ref = g.at[t, :, c]
        return copy(ref, ref, sib_s.at[t], sib_r.at[t], sibling)

    def sib_last(k):
        ref = chunk(y_block(0, 4), k)
        return copy(ref, ref, last_s.at[k], last_r.at[k], sibling)

    def hcopy(d, s):
        ref = hb.at[x_block(d, s)]
        src = ht if s == 0 else ref
        return copy(src, ref, h_s.at[d, s], h_r.at[d, s], x_long if d == 0 else x_short)

    steps = (4, 3)

    def h_step(s):
        for d in (0, 1):
            if s < steps[d]:
                hcopy(d, s).wait_recv()
                if s + 1 < steps[d]:
                    start(hcopy(d, s + 1))

    def sent(d, s, k):
        return s < 3 or (s == 3 and d == k // 2)

    def forward(s, k):
        for d in (0, 1):
            if sent(d, s, k):
                ring(d, s, k).wait_recv()
                if sent(d, s + 1, k):
                    start(ring(d, s + 1, k))

    perm = copy(gt, g.at[x, lax.rem(y, 4), c], perm_s, perm_r, perm_to)
    start(perm)

    loads[0].wait()
    loads[1].wait()
    for b in range(WCOL // BLK):
        cols = slice(b * BLK, (b + 1) * BLK)
        scale = jnp.broadcast_to(sv[b : b + 1, :], (BLK, FFD)).T
        w[h, :, cols] = (cv[:, cols].astype(F32) * scale).astype(BF16)

    def zcopy(k):
        ref = chunk(y, 0)
        return copy(ref, ref, z_s.at[k - 1], z_r.at[k - 1], z_peer[k - 1])

    perm.wait_recv()
    for r in range(1, 4):
        start(zcopy(r))
    for k in range(4):
        if k > 0:
            zcopy(k).wait_recv()
        start(ring(0, 0, k))
        start(ring(1, 0, k))
        if k == 0:
            for d in (0, 1):
                start(hcopy(d, 0))
    start(sib(y))
    w_copy = copy(w.at[h], w.at[h], w_s, w_r, h_peer)
    start(w_copy)
    h_step(0)

    def grad_hidden(t):
        r = lax.dot_general(
            w[0], g[t, 0:2].reshape(WCOL, TOK), (((1,), (0,)), ((), ())), preferred_element_type=F32
        )
        p[t] = r + lax.dot_general(
            w[1], g[t, 2:4].reshape(WCOL, TOK), (((1,), (0,)), ((), ())), preferred_element_type=F32
        )

    def grad_weight(t, first=False):
        for n in range(2):
            r = lax.dot_general(
                hb[t],
                g[t, 2 * n : 2 * n + 2].reshape(WCOL, TOK),
                (((1,), (1,)), ((), ())),
                preferred_element_type=F32,
            )
            if first:
                acc[n] = r
            else:
                acc[n] += r

    def at_distance(s):
        return [y_block(0, s)] if s in (0, 4) else [y_block(0, s), y_block(1, s)]

    half = FFD // 2

    def block_of(idx):
        b = mod(y + (idx + 1) // 2 * (1 if idx % 2 else -1), Y)
        return b, lax.rem(sgn * (b - x) + 2 * X, X)

    def rs(b, r, q, dst, recv, to):
        rows = pl.ds(q * half, half)
        return copy(rs_out.at[b, rows], dst.at[rows], rs_s.at[b, q], recv.at[q], to)

    def to_next(b, r, q):
        nx = mod(x + jnp.where(r <= 4, sgn, -sgn), X)
        return rs(b, r, q, pair_in.at[b], pair_r.at[b], dev(nx, h, zl, y, c))

    def to_owner(b, r, q):
        j = jnp.where(r == 3, 0, jnp.where(r == 6, 1, jnp.where(r == 1, 2, 3)))
        return rs(b, r, q, own_in.at[j], own_r.at[j], dev(b, h, zl, y, c))

    def launch(idx):
        b, r = block_of(idx)
        hand = (r == 4) | (r == 2) | (r == 5)
        for q in range(2):
            rows = pl.ds(q * half, half)

            @pl.when(hand | (r == 7))
            def _():
                rs_out[b, rows] = p[b, rows].astype(BF16)

            @pl.when(hand)
            def _():
                to_next(b, r, q).start()

            @pl.when(r == 7)
            def _():
                to_owner(b, r, q).start()

    def combine(idx):
        b, r = block_of(idx)

        @pl.when((r == 3) | (r == 1) | (r == 6))
        def _():
            for q in range(2):
                rows = pl.ds(q * half, half)
                to_next(b, r, q).wait_recv()
                rs_out[b, rows] = (p[b, rows] + pair_in[b, rows].astype(F32)).astype(BF16)
                to_owner(b, r, q).start()

    for s in range(4):
        for k in range(4):
            forward(s, k)
            if s == 3:
                start(sib_last(k))
        for t in at_distance(s + 1) if s < 3 else []:
            start(sib(t))
        if s < 3:
            h_step(s + 1)
        if s == 1:
            w_copy.wait_recv()
            for t in at_distance(0) + at_distance(1):
                sib(t).wait_recv()
                grad_hidden(t)
            for idx in (0, 1, 2):
                launch(idx)
        if s >= 2:
            for t in at_distance(s):
                sib(t).wait_recv()
                grad_hidden(t)
            for idx in (2 * s - 1, 2 * s):
                launch(idx)
        if s == 2:
            loads[2].wait()
            grad_weight(y, True)
            for t in at_distance(1) + at_distance(2):
                grad_weight(t)
        if s == 3:
            for idx in (0, 1, 2):
                combine(idx)
            for t in at_distance(3):
                grad_weight(t)
    last = y_block(0, 4)
    for k in range(4):
        sib_last(k).wait_recv()
    grad_hidden(last)
    launch(7)
    grad_weight(last)
    gw_out[...] = acc[1 - h].astype(BF16)
    gw_copy = copy(gw_out, gw_in, gw_s, gw_r, h_peer)
    start(gw_copy)
    for idx in (3, 4, 5, 6, 7):
        combine(idx)
    for q in range(2):
        rows = pl.ds(q * half, half)
        v = p[x, rows]
        for j in (3, 2, 1, 0):
            rs(x, 0, q, own_in.at[j], own_r.at[j], x_long).wait_recv()
            v = v + own_in[j, rows].astype(F32)
        ght[rows] = v.astype(BF16)
    gw_copy.wait_recv()
    gw[...] = acc[h] + gw_in[...].astype(F32)

    for idx in range(8):
        b, r = block_of(idx)

        @pl.when(r > 0)
        def _():
            for q in range(2):
                to_next(b, r, q).wait_send()

    for cp in sends:
        cp.wait_send()


def shards(hidden, grad_out, codes, scales):
    vmem = pl.BlockSpec(memory_space=pltpu.VMEM)
    hbm = pl.BlockSpec(memory_space=pltpu.HBM)
    dma = pltpu.SemaphoreType.DMA
    ght, gw = pl.pallas_call(
        kernel,
        out_shape=(
            jax.ShapeDtypeStruct((FFD, TOK), BF16),
            jax.ShapeDtypeStruct((FFD, WCOL), F32),
        ),
        in_specs=[hbm] * 4,
        out_specs=(vmem, vmem),
        scratch_shapes=[
            pltpu.VMEM((Y, 4, 2, GCOL, TOK), BF16),
            pltpu.VMEM((X, FFD, TOK), BF16),
            pltpu.VMEM((FFD, WCOL), BF16),
            pltpu.VMEM((WCOL // BLK, FFD), F32),
            pltpu.VMEM((2, FFD, WCOL), BF16),
            pltpu.VMEM((2, FFD, WCOL), F32),
            pltpu.VMEM((X, FFD, TOK), F32),
            pltpu.VMEM((X, FFD, TOK), BF16),
            pltpu.VMEM((X, FFD, TOK), BF16),
            pltpu.VMEM((4, FFD, TOK), BF16),
            pltpu.VMEM((FFD, WCOL), BF16),
            pltpu.VMEM((FFD, WCOL), BF16),
            dma((3,)),
            dma, dma,
            dma((3,)), dma((3,)),
            dma((2, 4, 4)), dma((2, 4, 4)),
            dma((8,)), dma((8,)),
            dma((4,)), dma((4,)),
            dma((2, 4)), dma((2, 4)),
            dma, dma,
            dma((X, 2)), dma((X, 2)), dma((4, 2)),
            dma, dma,
        ],
        compiler_params=pltpu.CompilerParams(
            collective_id=0, has_side_effects=True, vmem_limit_bytes=32 * 2**20
        ),
        name="fused",
    )(*[pltpu.with_memory_space_constraint(v, pltpu.HBM) for v in (hidden.T, grad_out.T, codes, scales.T)])
    return ght.T, gw


def solution(mesh):
    return jax.shard_map(
        shards,
        mesh=mesh,
        in_specs=(
            P("inner", "outer"),
            P("inner", "outer"),
            P("outer", "inner"),
            P("outer", "inner"),
        ),
        out_specs=(P("inner", "outer"), P("outer", "inner")),
        check_vma=False,
    )
```

time: 83.5 us -> 72.5 us (0.87)
  the two profiles are of different devices: /device:TPU:2 before, /device:TPU:450 now
where the time goes in v2:
time: 72.5 us; the launch traced here: 72.4 us
  Pallas kernels  70.3 us (97%)
  local copies, waits for them, and re-layouts  1.38 us (2%)
    pallas_call x1, Pallas kernels, shards(): pl.pallas_call(kernel, out_shape=(jax.ShapeDtypeStruct((FFD, TOK), BF16),...  70.3 us

profile of v2, /device:TPU:450, one launch (start us, length us, event | category | flops | bytes accessed | tf_op | source)
XLA Modules:
  0.0 72.4 jit_solution(10929837697020501559)
XLA Ops:
  0.6 70.3 %fused.1 = (bf16[224,256]{1,0:T(8,128)(2,1)S(1)}, f32[224,384]{1,0:T(8,128)S(1)}) custom-call(bf16[224,256]{1,0:T(8,128)(2,1)} %bitcast.5, bf16[96,256]{1,0:T(8,128)(2,1)} %bitcast.6, bf16[224,384]{1,0:T(8,128)(2,1)} %codes.1, f32[3,224]{1,0:T(4,128)} %bitcast.7), custom_call_target="tpu_custom_call" | custom-call | tf_op jit(solution)/shard_map/fused/pallas_call | solution.py:285
  71.0 0.6 copy.8
  71.6 0.7 %copy.9 = f32[224,384]{1,0:T(8,128)} copy(f32[224,384]{1,0:T(8,128)S(1)} %get-tuple-element.9) | data formatting | bytes 688128

commit v3 on v2

--- a/solution.py
+++ b/solution.py
@@ -241,19 +241,19 @@
             for t in at_distance(1) + at_distance(2):
                 grad_weight(t)
         if s == 3:
+            for t in at_distance(3):
+                grad_weight(t)
             for idx in (0, 1, 2):
                 combine(idx)
-            for t in at_distance(3):
-                grad_weight(t)
     last = y_block(0, 4)
     for k in range(4):
         sib_last(k).wait_recv()
-    grad_hidden(last)
-    launch(7)
     grad_weight(last)
     gw_out[...] = acc[1 - h].astype(BF16)
     gw_copy = copy(gw_out, gw_in, gw_s, gw_r, h_peer)
     start(gw_copy)
+    grad_hidden(last)
+    launch(7)
     for idx in (3, 4, 5, 6, 7):
         combine(idx)
     for q in range(2):

time: 72.5 us -> 72.5 us (level)
  no operation moved by 1% of the time
where the time goes in v3:
time: 72.5 us; the launch traced here: 72.4 us
  Pallas kernels  70.4 us (97%)
  local copies, waits for them, and re-layouts  1.38 us (2%)
    pallas_call x1, Pallas kernels, shards(): pl.pallas_call(kernel, out_shape=(jax.ShapeDtypeStruct((FFD, TOK), BF16),...  70.4 us

profile of v3, /device:TPU:450, one launch (start us, length us, event | category | flops | bytes accessed | tf_op | source)
XLA Modules:
  0.0 72.4 jit_solution(18186807898089435685)
XLA Ops:
  0.6 70.4 %fused.1 = (bf16[224,256]{1,0:T(8,128)(2,1)S(1)}, f32[224,384]{1,0:T(8,128)S(1)}) custom-call(bf16[224,256]{1,0:T(8,128)(2,1)} %bitcast.5, bf16[96,256]{1,0:T(8,128)(2,1)} %bitcast.6, bf16[224,384]{1,0:T(8,128)(2,1)} %codes.1, f32[3,224]{1,0:T(4,128)} %bitcast.7), custom_call_target="tpu_custom_call" | custom-call | tf_op jit(solution)/shard_map/fused/pallas_call | solution.py:285
  71.0 0.6 copy.8
  71.6 0.7 %copy.9 = f32[224,384]{1,0:T(8,128)} copy(f32[224,384]{1,0:T(8,128)S(1)} %get-tuple-element.9) | data formatting | bytes 688128
